TPU v7x, 512 devices: a whole 4x8x8 slice. The times are simulated.
512 devices in a mesh: row: 32 (over x, y_lo, core), col: 16 (over y_hi, z).
Axes of the slice: x: 4, y: 8 (y_hi: 2, y_lo: 4; y = y_hi * 4 + y_lo), z: 8, core: 2. Of those that a mesh axis runs over, the one named last changes fastest.
Arguments:
- amps: bfloat16 [800, 800, 256], P('col', 'row'), may hold values from -6 to 6
- integral: bfloat16 [800, 800, 256], P('row', 'col'), may hold values from -0.078125 to 0.078125
- virt_irrep: int32 [8], replicated, may hold values from 0 to 7
- occ_irrep: int32 [64], replicated, may hold values from 0 to 7
Outputs:
- resid: float32 [800, 4, 3200], P('row', None, 'col')
Inputs may be any that keep to these rules, and one draw needn't show every extreme that they name: `virt_irrep`: labels of the eight D2h irreducible representations. `occ_irrep`: labels of the eight D2h irreducible representations.
All inputs are finite; a program needn't handle non-finite values.
Results may differ from a plain program's by a relative error of at most 0.005.
Values may be sent and summed in bfloat16 or wider, within the bound.
A program may use at most 128 MiB of HBM per device.

v0:
```python
import jax
import jax.numpy as jnp
from jax import lax
from jax.sharding import PartitionSpec as P

VBLK = 100


def broadcast(array, axis, root):
    mine = lax.axis_index(axis) == root
    return lax.psum(jnp.where(mine, array, jnp.zeros_like(array)), axis)


def irrep_of(table, positions):
    blocks = positions // VBLK
    onehot = blocks[:, None] == jnp.arange(table.shape[0], dtype=jnp.int32)[None, :]
    return jnp.sum(jnp.where(onehot, table[None, :], 0), axis=1)


def antisym_pairs(partial_cycle, window, b_count):
    rows_here = partial_cycle.shape[0]
    four_way = partial_cycle.reshape(rows_here, window, b_count, window)
    paired = four_way - four_way.transpose(0, 3, 2, 1)
    return paired.reshape(rows_here, window, b_count * window).astype(jnp.bfloat16)


def shards(amps, integral, virt_irrep, occ_irrep):
    p_count, q_count, last_width = amps.shape
    c_count, b_count, _ = integral.shape
    occ_count = occ_irrep.shape[0]
    window = last_width // occ_count
    row_id = lax.axis_index("row")
    col_id = lax.axis_index("col")
    row_size = lax.axis_size("row")
    window_label = occ_irrep[:window]
    p_label = irrep_of(virt_irrep, col_id * p_count + jnp.arange(p_count, dtype=jnp.int32))
    q_label = irrep_of(virt_irrep, row_id * q_count + jnp.arange(q_count, dtype=jnp.int32))
    amp_keep = (
        jnp.bitwise_xor(
            jnp.bitwise_xor(p_label[:, None, None, None], q_label[None, :, None, None]),
            jnp.bitwise_xor(window_label[None, None, :, None], occ_irrep[None, None, None, :]),
        )
        == 0
    )
    amp_four = amps.reshape(p_count, q_count, window, occ_count)
    amp_masked = jnp.where(amp_keep, amp_four, jnp.zeros_like(amp_four)).reshape(
        p_count, q_count, last_width
    )
    c_label = irrep_of(virt_irrep, row_id * c_count + jnp.arange(c_count, dtype=jnp.int32))
    b_label = irrep_of(virt_irrep, col_id * b_count + jnp.arange(b_count, dtype=jnp.int32))
    int_keep = (
        jnp.bitwise_xor(
            jnp.bitwise_xor(c_label[:, None, None, None], b_label[None, :, None, None]),
            jnp.bitwise_xor(occ_irrep[None, None, :, None], window_label[None, None, None, :]),
        )
        == 0
    )
    int_four = integral.reshape(c_count, b_count, occ_count, window)
    int_masked = jnp.where(int_keep, int_four, jnp.zeros_like(int_four))
    piece = lax.all_gather(amp_masked, "col", axis=0, tiled=True)
    piece_rows = piece.shape[0]
    piece_four = piece.reshape(piece_rows, q_count, window, occ_count)
    product = lax.dot_general(
        piece_four, int_masked, (((1, 3), (0, 2)), ((), ())), preferred_element_type=jnp.float32
    )
    partial_cycle = product.reshape(piece_rows, window, b_count * window)
    a_count = partial_cycle.shape[0] // row_size
    column_pair = None
    own_cycle = lax.psum_scatter(partial_cycle, "row", scatter_dimension=0, tiled=True)
    own_pair = antisym_pairs(own_cycle, window, b_count)
    own_tile = own_pair.reshape(a_count, window, b_count, window)
    column_pair = lax.all_gather(own_pair, "row", axis=0, tiled=True)
    total_rows = column_pair.shape[0]
    column_four = column_pair.reshape(total_rows, window, b_count, window)
    first_a = row_id * a_count
    inner_start = first_a % b_count
    root_col = first_a // b_count
    slice_out = lax.dynamic_slice_in_dim(column_four, inner_start, a_count, 2)
    received = broadcast(slice_out, "col", root_col)
    mirror_piece = lax.dynamic_slice_in_dim(received, col_id * b_count, b_count, 0)
    mirror_tile = mirror_piece.transpose(2, 1, 0, 3).astype(jnp.float32)
    own_four = own_tile.astype(jnp.float32)
    resid = own_four - mirror_tile
    return resid.reshape(a_count, window, b_count * window)


def solution(mesh):
    placed = (P("col", "row", None), P("row", "col", None), P(), P())
    return jax.shard_map(
        shards, mesh=mesh, in_specs=placed, out_specs=P("row", None, "col"), check_vma=False
    )
```

profile of v0, /device:TPU:7, one launch (start us, length us, event | category | flops | bytes accessed | tf_op | source)
XLA Modules:
  0.0 921.0 jit_solution(8601381485628055920)
XLA Ops:
  6.5 0.0 copy-start.2
  6.5 0.0 all-gather.3.cloned.1.call-start
  6.5 0.8 broadcast_reduce_fusion
  7.3 0.1 xor.108
  7.4 0.7 xor.109
  8.1 0.1 xor.110
  8.2 0.7 select_reduce_fusion
  9.0 0.7 select_reduce_fusion.1
  9.7 0.1 broadcast_xor_fusion.1
  9.8 2.4 fusion.2
  12.1 0.0 all-gather.3.cloned.1.call-update
  12.2 0.0 all-reduce.6.cloned.1.call-start
  12.2 1.9 copy.32
  14.2 0.1 broadcast_xor_fusion.2
  14.2 0.0 copy-done.2
  14.2 0.1 broadcast_xor_fusion
  14.3 1.2 fusion.1
  15.5 2.9 copy.33
  18.4 270.9 %all-gather.3.cloned.1.call-done = bf16[800,25,256]{2,1,0:T(8,128)(2,1)} async-done(((bf16[50,25,256]{2,1,0:T(8,128)(2,1)}), bf16[800,25,256]{2,1,0:T(8,128)(2,1)}) %all-gather.3.cloned.1.call-update) | async-done | bytes 10240016 | tf_op jit(solution)/shard_map/all_gather | solution.py:60
  289.3 20.9 %copy.31 = bf16[800,25,256]{0,2,1:T(8,128)(2,1)} copy(bf16[800,25,256]{2,1,0:T(8,128)(2,1)} %all-gather.3.cloned.1.call-done) | data formatting | bytes 20480000 | tf_op jit(solution)/shard_map/all_gather | solution.py:60
  310.2 6.2 convolution_bitcast_fusion
  316.5 2.9 copy.35
  319.4 0.0 all-reduce.6.cloned.1.call-update
  319.4 0.0 all-gather.5.cloned.1.call-start
  319.5 1.3 dynamic-slice
  321.4 273.7 %all-reduce.6.cloned.1.call-done = f32[800,4,200]{2,1,0:T(4,128)} async-done(((f32[800,4,200]{2,1,0:T(4,128)}), f32[800,4,200]{2,1,0:T(4,128)}) %all-reduce.6.cloned.1.call-update) | async-done | bytes 2560016
  595.1 0.9 constant_dynamic-slice_fusion
  596.0 0.2 copy.36
  596.2 0.0 copy-start
  596.2 0.1 fusion.3
  596.4 0.8 copy.38
  597.2 0.0 all-gather.5.cloned.1.call-update
  597.2 0.0 all-reduce.4.cloned.1.call-start
  597.3 72.7 %all-gather.5.cloned.1.call-done = bf16[800,4,200]{2,1,0:T(4,128)(2,1)} async-done(((bf16[25,4,200]{2,1,0:T(4,128)(2,1)}), bf16[800,4,200]{2,1,0:T(4,128)(2,1)}) %all-gather.5.cloned.1.call-update) | async-done | bytes 1280016 | tf_op jit(solution)/shard_map/all_gather | solution.py:72
  670.0 4.4 copy.39
  674.4 0.0 copy-done
  674.5 1.1 constant_dynamic-slice_fusion.1
  675.6 5.6 copy.48
  681.2 3.0 broadcast_select_fusion
  684.2 0.0 copy-start.1
  684.2 0.0 all-reduce.4.cloned.1.call-update
  684.3 228.2 %all-reduce.4.cloned.1.call-done = bf16[800,4,25,4]{2,3,0,1:T(4,128)(2,1)} async-done(((bf16[800,4,25,4]{2,3,0,1:T(4,128)(2,1)}), bf16[800,4,25,4]{2,3,0,1:T(4,128)(2,1)}) %all-reduce.4.cloned.1.call-update) | async-done | bytes 640016 | tf_op jit(solution)/shard_map/psum | solution.py:11
  912.5 0.0 copy-done.1
  912.5 1.1 bitcast_subtract_fusion
  913.6 0.8 copy.41
  (3 shorter events, 0.0 us)
Async XLA Ops:
  6.5 7.7 copy-start.2
  6.5 282.8 %all-gather.3.cloned.1.call-start = ((), (), s32[]{:S(2)}) async-start(), calls=%async_computation | async-start | bytes 13926400 | tf_op jit(solution)/shard_map/all_gather | solution.py:60
  12.2 583.0 %all-reduce.6.cloned.1.call-start = ((), (), s32[]{:S(2)}) async-start(), calls=%async_computation.3 | async-start | bytes 6553600
  319.4 350.6 %all-gather.5.cloned.1.call-start = ((), (), s32[]{:S(2)}) async-start(), calls=%async_computation.1 | async-start | bytes 1689600 | tf_op jit(solution)/shard_map/all_gather | solution.py:72
  596.2 78.2 %copy-start = (f32[25,4,200]{0,2,1:T(8,128)}, f32[25,4,200]{0,2,1:T(8,128)S(1)}, u32[]{:S(2)}) copy-start(f32[25,4,200]{0,2,1:T(8,128)S(1)} %copy.36) | copy-start | bytes 240004
  597.2 315.3 %all-reduce.4.cloned.1.call-start = ((), (), s32[]{:S(2)}) async-start(), calls=%async_computation.2 | async-start | bytes 6553600 | tf_op jit(solution)/shard_map/psum | solution.py:11
  684.2 228.3 %copy-start.1 = (f32[25,4,200]{0,2,1:T(8,128)S(1)}, f32[25,4,200]{0,2,1:T(8,128)}, u32[]{:S(2)}) copy-start(f32[25,4,200]{0,2,1:T(8,128)} %copy-done) | copy-start | bytes 240004
Sparse Core Ops, SparseCore 0:
  12.3 276.9 all-gather.2
  319.5 275.5 all-reduce.5
  597.5 72.4 all-gather.4
  684.4 228.0 all-reduce.3
where the time goes:
time: 926 us; the launch traced here: 921 us
  waiting for transfers between devices  846 us (91%)
  local copies, waits for them, and re-layouts  45.5 us (5%)
  between operations  13.9 us (2%)
  other arithmetic  9.59 us (1%)
    unnamed x5, waiting for transfers between devices  274 us
    all_gather x1, waiting for transfers between devices, shards(): piece = lax.all_gather(amp_masked, 'col', axis=0, tiled=True)  271 us
    psum x1, waiting for transfers between devices, broadcast(): return lax.psum(jnp.where(mine, array, jnp.zeros_like(array)), axis)  228 us
    all_gather x1, waiting for transfers between devices, shards(): column_pair = lax.all_gather(own_pair, 'row', axis=0, tiled=True)  72.7 us
    all_gather x1, local copies, waits for them, and re-layouts, shards(): piece = lax.all_gather(amp_masked, 'col', axis=0, tiled=True)  20.9 us
  transfers between devices with their start and end apart: 4, of which 4 were waited for; matrix products, arithmetic and copies ran while one was open for 1% of the time, Pallas kernels for 0%

commit v1 on v0

v1 whole, which is shorter than its diff:
```python
import functools

import jax
import jax.numpy as jnp
from jax import lax
from jax.experimental import pallas as pl
from jax.experimental.pallas import tpu as pltpu
from jax.sharding import PartitionSpec as P

MESH = pl.DeviceIdType.MESH
F32 = jnp.float32
BF16 = jnp.bfloat16
I32 = jnp.int32

NP = 50
NQ = 25
OW = 4
NO = 64
PAIRS = ((0, 1), (0, 2), (0, 3), (1, 2), (1, 3), (2, 3))
ROWS = 208
CUT = 112
SLOT = 64
MSG = len(PAIRS) * SLOT
ZN = 8
YH = 2


def iota(shape, dim):
    return lax.broadcasted_iota(I32, shape, dim)


def dot(a, b, dims):
    return lax.dot_general(a, b, (dims, ((), ())), preferred_element_type=F32)


NN = ((1,), (0,))
NT = ((1,), (1,))
TN = ((0,), (0,))


def kernel(cap, amps, integral, occ_row, occ, virt, out, ta, t32, tg, wall, st, sw, c32, keep, psend, precv, msg, p2r,
           zmat, tile, p3r, ag_s, ag_r, w_s, w_r, d_s, d_r, p2_s, p2_rs, p3_s, p3_rs, loc):
    group = 128 // cap
    tiles = -(-NQ // group)
    row = lax.axis_index("row")
    col = lax.axis_index("col")
    core = row % 2
    chip = row // 2
    yh = col // ZN
    z = col % ZN

    bar = pltpu.get_barrier_semaphore()

    def signal(r, c):
        pl.semaphore_signal(bar, inc=1, device_id=(r, c), device_id_type=MESH)

    right = yh * ZN + (z + 1) % ZN
    left = yh * ZN + (z + ZN - 1) % ZN
    opposite = (1 - yh) * ZN + z
    mate = row + 1 - 2 * core
    signal(row, right)
    signal(row, left)
    signal(row, opposite)
    signal(mate, col)
    home = chip // ZN

    def greet(n, carry):
        @pl.when(jnp.logical_not((n == chip) & (home == yh)))
        def _():
            signal(2 * n + core, home * ZN + z)

        return carry

    lax.fori_loop(0, 16, greet, 0)
    mirror_col = row // 2
    for s in range(2):
        @pl.when(jnp.logical_not((2 * col + s == row) & (mirror_col == col)))
        def _():
            signal(2 * col + s, mirror_col)

    own_p2 = (home == yh).astype(I32)
    own_p3 = (mirror_col == col).astype(I32)

    block_label = virt[col // 2] ^ virt[row // 4]
    lab = occ_row[...].astype(F32)
    wide = (256, NO)
    r256, l64 = iota(wide, 0), iota(wide, 1)

    def column(which):
        return jnp.sum(jnp.where(l64 == which, lab, 0.0), axis=1, keepdims=True)

    lane = iota((1, group * 128 * 4 // group), 1)
    lane_slot = lane % 128
    lane_key = (lane // 128) * 128 + lane_slot % cap
    lane_group = lane_slot // cap

    def select(ref, k_of, i_of):
        hk = column(k_of)
        hi = column(i_of)
        keep_it = (hk.astype(I32) ^ hi.astype(I32)) == block_label
        if cap == NO:
            place = k_of[:, :1]
        else:
            same = (lab == hk) & (l64 < k_of)
            place = jnp.sum(jnp.where(same, 1.0, 0.0), axis=1, keepdims=True).astype(I32)
        key = jnp.where(keep_it, i_of[:, :1] * 128 + place, -1)
        for g in range(group):
            hit = (key == lane_key) & (lane_group == g)
            ref[g * 256:(g + 1) * 256, :] = jnp.where(hit, 1.0, 0.0).astype(BF16)

    select(st, r256 % NO, r256 // NO)

    def widen(a, carry):
        plane = amps[a].astype(F32)
        for u in range(2):
            ta[u, pl.ds(pl.multiple_of(a * 32, 32), NQ), :] = plane[:, u * 128:(u + 1) * 128]
        return carry

    lax.fori_loop(0, NP, widen, 0, unroll=5)
    t32[OW * NP:ROWS, :] = jnp.zeros((ROWS - OW * NP, tiles * 128), F32)
    for q in range(tiles):
        cs = range(q * group, min(NQ, (q + 1) * group))
        x = jnp.concatenate([ta[u, pl.ds(c, NP, stride=32), :].astype(BF16) for c in cs for u in range(2)], axis=1)
        y = dot(x, st[0:len(cs) * 256, :], NN)
        for i in range(OW):
            t32[i * NP:(i + 1) * NP, q * 128:(q + 1) * 128] = y[:, i * 128:(i + 1) * 128]
    tg[z] = t32[...].astype(BF16)

    pl.semaphore_wait(bar, 22 - own_p2 - own_p3)

    parts = ((0, CUT), (CUT, ROWS - CUT))

    def hop(direction, step, part):
        src = (z + ZN - step) % ZN if direction == 0 else (z + step) % ZN
        lo, size = parts[part]
        n = (direction * 4 + step) * 2 + part
        return pltpu.make_async_remote_copy(
            src_ref=tg.at[src, pl.ds(lo, size)], dst_ref=tg.at[src, pl.ds(lo, size)], send_sem=ag_s.at[n], recv_sem=ag_r.at[n],
            device_id=(row, right if direction == 0 else left), device_id_type=MESH)

    def arrival(direction, step, part):
        src = (z + ZN - step - 1) % ZN if direction == 0 else (z + step + 1) % ZN
        lo, size = parts[part]
        n = (direction * 4 + step) * 2 + part
        return pltpu.make_async_remote_copy(
            src_ref=tg.at[src, pl.ds(lo, size)], dst_ref=tg.at[src, pl.ds(lo, size)], send_sem=ag_s.at[n], recv_sem=ag_r.at[n],
            device_id=(row, right if direction == 0 else left), device_id_type=MESH)

    for part in range(2):
        for d in range(2):
            hop(d, 0, part).start()

    select(sw, r256 // OW, r256 % OW)
    for q in range(tiles):
        cs = range(q * group, min(NQ, (q + 1) * group))
        x = jnp.concatenate([integral[c] for c in cs], axis=1)
        y = dot(x, sw[0:len(cs) * 256, :], NN)
        y = jnp.concatenate([y, jnp.zeros((SLOT - NP, 512), F32)], axis=0).astype(BF16)
        for j in range(OW):
            wall[yh, j * SLOT:(j + 1) * SLOT, q * 128:(q + 1) * 128] = y[:, j * 128:(j + 1) * 128]
    swap = pltpu.make_async_remote_copy(
        src_ref=wall.at[yh], dst_ref=wall.at[yh], send_sem=w_s, recv_sem=w_r, device_id=(row, opposite), device_id_type=MESH)
    swap_in = pltpu.make_async_remote_copy(
        src_ref=wall.at[1 - yh], dst_ref=wall.at[1 - yh], send_sem=w_s, recv_sem=w_r, device_id=(row, opposite), device_id_type=MESH)
    swap.start()

    zr, zl = iota((MSG, OW * 256), 0), iota((MSG, OW * 256), 1)
    zp, zb = zr // SLOT, zr % SLOT
    zi, zt = zl // 256, zl % 256
    first = jnp.where(zp < 3, 0, jnp.where(zp < 5, 1, 2))
    second = jnp.where(zp < 3, zp + 1, jnp.where(zp < 5, zp - 1, 3))
    here = (zt // OW == zb) & (zb < NP)
    plus = here & (zi == first) & (zt % OW == second)
    minus = here & (zi == second) & (zt % OW == first)
    zmat[...] = (jnp.where(plus, 1.0, 0.0) - jnp.where(minus, 1.0, 0.0)).astype(BF16)

    low = iota((32, 128), 1) < SLOT

    def mate_copy(n):
        return pltpu.make_async_remote_copy(
            src_ref=psend.at[n], dst_ref=precv.at[n], send_sem=d_s.at[n], recv_sem=d_r.at[n], device_id=(mate, col),
            device_id_type=MESH)

    def compute(n, off):
        za = (z + off) % ZN
        for h in range(YH):
            c32[:, h * 256:(h + 1) * 256] = dot(tg[za], wall[h], NT)
        la = virt[(yh * ZN + za) // 2]
        halves = []
        for half in range(2):
            line = []
            for h in range(YH):
                lb = virt[(h * ZN + z) // 2]
                for t in range(3):
                    both = []
                    for p in (2 * t, 2 * t + 1):
                        i, j = PAIRS[p]

                        def piece(r, s):
                            start = NP * r + NQ * half
                            v = c32[start:start + 32, h * 256 + (s // 2) * 128:h * 256 + (s // 2) * 128 + 128]
                            return v if s % 2 == p % 2 else pltpu.roll(v, SLOT, axis=1)

                        scale = jnp.where((la ^ lb ^ occ[i] ^ occ[j]) == 0, 1.0, 0.0)
                        both.append((piece(i, j) - piece(j, i)) * scale)
                    line.append(jnp.where(low, both[0], both[1]))
            halves.append(jnp.concatenate(line, axis=1))
        keep[n] = jnp.where(core == 0, halves[0], halves[1])
        psend[n] = jnp.where(core == 0, halves[1], halves[0]).astype(BF16)
        mate_copy(n).start()

    def finish(n, off):
        za = (z + off) % ZN
        mate_copy(n).wait_recv()
        total = (keep[n] + precv[n].astype(F32)).astype(BF16)
        for h in range(YH):
            msg[n, h] = total[:, h * MSG:(h + 1) * MSG]
            to_row = 2 * (yh * ZN + za) + core
            mine = (to_row == row) & (yh == h)

            @pl.when(jnp.logical_not(mine))
            def _():
                pltpu.make_async_remote_copy(
                    src_ref=msg.at[n, h], dst_ref=p2r.at[chip], send_sem=p2_s, recv_sem=p2_rs,
                    device_id=(to_row, h * ZN + z), device_id_type=MESH).start()

            @pl.when(mine)
            def _():
                pltpu.make_async_copy(msg.at[n, h], p2r.at[chip], p2_rs).start()

    order = (0, ZN - 1, 1, ZN - 2, 2, ZN - 3, 3, 4)
    for step in range(1, 4):
        for part in range(2):
            for d in range(2):
                arrival(d, step - 1, part).wait_recv()
                if step < 3 or part == d:
                    hop(d, step, part).start()
        if step == 2:
            swap_in.wait_recv()
            for n in range(5):
                compute(n, order[n])
            for n in range(5):
                finish(n, order[n])
        if step == 3:
            for n in (5, 6):
                compute(n, order[n])
            for n in (5, 6):
                finish(n, order[n])
    for d in range(2):
        arrival(d, 3, d).wait_recv()
    compute(7, order[7])
    finish(7, order[7])

    pltpu.make_async_copy(p2r, p2r, p2_rs).wait()
    total = p2r[0].astype(F32)
    for n in range(1, 16):
        total = total + p2r[n].astype(F32)
    tile[...] = total.astype(BF16)

    def mirror_copy(s):
        return pltpu.make_async_remote_copy(
            src_ref=tile, dst_ref=p3r.at[row % 2], send_sem=p3_s.at[s], recv_sem=p3_rs.at[row % 2],
            device_id=(2 * col + s, mirror_col), device_id_type=MESH)

    for s in range(2):
        self_mirror = (2 * col + s == row) & (mirror_col == col)

        @pl.when(jnp.logical_not(self_mirror))
        def _():
            mirror_copy(s).start()

        @pl.when(self_mirror)
        def _():
            pltpu.make_async_copy(tile, p3r.at[s], p3_rs.at[s]).start()

    base = dot(tile[...], zmat[...], NN)
    er, el = iota((32, 256), 0), iota((32, 256), 1)
    spread = None
    for s in range(2):
        pltpu.make_async_copy(p3r.at[s], p3r.at[s], p3_rs.at[s]).wait()
        put = ((el % 128) == er + NQ * s + SLOT * (el // 128)) & (er < NQ)
        part = dot(p3r[s], jnp.where(put, 1.0, 0.0).astype(BF16), TN)
        spread = part if spread is None else spread + part
    line = []
    for t in range(3):
        both = []
        for u in range(2):
            lo = (2 * t + u) * SLOT
            a0 = spread[lo:lo + 32, u * 128:(u + 1) * 128]
            a1 = spread[lo + NQ:lo + NQ + 32, u * 128:(u + 1) * 128]
            both.append(jnp.where(row % 2 == 0, a0, a1))
        line.append(both[0] + both[1])
    swapped = jnp.concatenate(line, axis=1).astype(BF16)
    res = base - dot(swapped, zmat[...], NN)
    for i in range(OW):
        out[i] = res[0:NQ, i * 256:i * 256 + NP * OW]

    for part in range(2):
        for d in range(2):
            for step in range(4):
                if step < 3 or part == d:
                    hop(d, step, part).wait_send()
    swap.wait_send()
    for n in range(8):
        mate_copy(n).wait_send()

    @pl.when(home == yh)
    def _():
        pltpu.make_async_copy(p2r.at[pl.ds(0, 15)], p2r.at[pl.ds(0, 15)], p2_s).wait()

    @pl.when(home != yh)
    def _():
        pltpu.make_async_copy(p2r, p2r, p2_s).wait()

    for s in range(2):
        @pl.when(jnp.logical_not((2 * col + s == row) & (mirror_col == col)))
        def _():
            mirror_copy(s).wait_send()


def call(cap, collective_id, amps, integral, virt_irrep, occ_irrep):
    group = 128 // cap
    lanes = -(-NQ // group) * 128
    vmem = pl.BlockSpec(memory_space=pltpu.VMEM)
    smem = pl.BlockSpec(memory_space=pltpu.SMEM)
    dma = pltpu.SemaphoreType.DMA
    return pl.pallas_call(
        functools.partial(kernel, cap),
        out_shape=jax.ShapeDtypeStruct((OW, NQ, NP * OW), F32),
        in_specs=[vmem, vmem, vmem, smem, smem],
        out_specs=vmem,
        scratch_shapes=[
            pltpu.VMEM((2, NP * 32, 128), F32),
            pltpu.VMEM((ROWS, lanes), F32),
            pltpu.VMEM((ZN, ROWS, lanes), BF16),
            pltpu.VMEM((YH, OW * SLOT, lanes), BF16),
            pltpu.VMEM((group * 256, 512), BF16),
            pltpu.VMEM((group * 256, 512), BF16),
            pltpu.VMEM((ROWS, 512), F32),
            pltpu.VMEM((ZN, 32, YH * MSG), F32),
            pltpu.VMEM((ZN, 32, YH * MSG), BF16),
            pltpu.VMEM((ZN, 32, YH * MSG), BF16),
            pltpu.VMEM((ZN, YH, 32, MSG), BF16),
            pltpu.VMEM((16, 32, MSG), BF16),
            pltpu.VMEM((MSG, OW * 256), BF16),
            pltpu.VMEM((32, MSG), BF16),
            pltpu.VMEM((2, 32, MSG), BF16),
            dma((16,)), dma((16,)), dma, dma, dma((ZN,)), dma((ZN,)), dma, dma, dma((2,)), dma((2,)), dma,
        ],
        name="cycle%d" % cap,
        compiler_params=pltpu.CompilerParams(
            collective_id=collective_id, has_side_effects=True, vmem_limit_bytes=48 * 2**20),
    )(amps, integral, occ_irrep.reshape(1, NO), occ_irrep, virt_irrep)


def shards(amps, integral, virt_irrep, occ_irrep):
    tile = call(NO, 0, amps, integral, virt_irrep, occ_irrep)
    return tile.transpose(1, 0, 2)


def solution(mesh):
    placed = (P("col", "row", None), P("row", "col", None), P(), P())
    return jax.shard_map(
        shards, mesh=mesh, in_specs=placed, out_specs=P("row", None, "col"), check_vma=False
    )
```

time: 926 us -> 92.9 us (0.10)
  waiting for transfers between devices: 846 us -> 0 us
  Pallas kernels: 0 us -> 90.7 us
  local copies, waits for them, and re-layouts: 45.5 us -> 2.07 us
  between operations: 13.9 us -> 0.04 us
  other arithmetic: 9.59 us -> 0 us
    all_gather x2 -> x0, waiting for transfers between devices: 344 us -> none  [the longest x1 271 us: shards(): piece = lax.all_gather(amp_masked, 'col', axis=0, tiled=True)]
    unnamed x5 -> x0, waiting for transfers between devices: 274 us -> none
    psum x1 -> x0, waiting for transfers between devices: 228 us -> none  [broadcast(): return lax.psum(jnp.where(mine, array, jnp.zeros_like(array)), axis)]
    pallas_call x0 -> x1, Pallas kernels: none -> 90.7 us  [call(): pl.pallas_call(functools.partial(kernel, cap), out_shape=jax.ShapeDtypeSt...]
    all_gather x2 -> x0, local copies, waits for them, and re-layouts: 25.4 us -> none  [the longest x1 20.9 us: shards(): piece = lax.all_gather(amp_masked, 'col', axis=0, tiled=True)]
  transfers between devices with their start and end apart: 4 -> 0, of which waited for: 4 -> 0; matrix products, arithmetic and copies ran while one was open for 1% -> 0% of each run, Pallas kernels for 0% -> 0%
where the time goes in v1:
time: 92.9 us; the launch traced here: 92.8 us
  Pallas kernels  90.7 us (98%)
  local copies, waits for them, and re-layouts  2.07 us (2%)
    pallas_call x1, Pallas kernels, call(): pl.pallas_call(functools.partial(kernel, cap), out_shape=jax.ShapeDtypeSt...  90.7 us

profile of v1, /device:TPU:7, one launch (start us, length us, event | category | flops | bytes accessed | tf_op | source)
XLA Modules:
  0.0 92.8 jit_solution(5039870202412490164)
XLA Ops:
  0.0 0.0 copy-start
  0.0 0.0 copy-start.1
  0.0 0.0 copy-start.2
  0.0 1.3 %copy.5.amps = bf16[50,25,256]{2,1,0:T(8,128)(2,1)S(1)} copy(bf16[50,25,256]{2,0,1:T(8,128)(2,1)} %param.4) | data formatting | bytes 1280000 | tf_op args[0]
  1.4 0.0 copy-done
  1.4 0.0 copy-done.1
  1.4 0.0 copy-done.2
  1.4 90.7 %cycle64.1 = f32[4,25,200]{2,1,0:T(8,128)S(1)} custom-call(bf16[50,25,256]{2,1,0:T(8,128)(2,1)S(1)} %copy.5.amps, bf16[25,50,256]{2,1,0:T(8,128)(2,1)S(1)} %copy-done, s32[1,64]{1,0:T(1,128)S(1)} %bitcast.3, s32[64]{0:T(128)S(1)} %copy-done.1, s32[8]{0:T(128)S(1)} %copy-done.2), custom_call_target="tpu_custom_call" | custom-call | tf_op jit(solution)/shard_map/cycle64/pallas_call | solution.py:327
  92.1 0.7 copy.6
Async XLA Ops:
  0.0 1.4 %copy-start = (bf16[25,50,256]{2,1,0:T(8,128)(2,1)S(1)}, bf16[25,50,256]{2,1,0:T(8,128)(2,1)}, u32[]{:S(2)}) copy-start(bf16[25,50,256]{2,1,0:T(8,128)(2,1)} %integral.1) | copy-start | bytes 1920004
  0.0 1.4 %copy-start.1 = (s32[64]{0:T(128)S(1)}, s32[64]{0:T(128)}, u32[]{:S(2)}) copy-start(s32[64]{0:T(128)} %occ.1) | copy-start | bytes 772
  0.0 1.4 %copy-start.2 = (s32[8]{0:T(128)S(1)}, s32[8]{0:T(128)}, u32[]{:S(2)}) copy-start(s32[8]{0:T(128)} %virt.1) | copy-start | bytes 100

commit v2 on v1

v2 whole, which is shorter than its diff:
```python
import functools

import jax
import jax.numpy as jnp
from jax import lax
from jax.experimental import pallas as pl
from jax.experimental.pallas import tpu as pltpu
from jax.sharding import PartitionSpec as P

MESH = pl.DeviceIdType.MESH
F32 = jnp.float32
BF16 = jnp.bfloat16
I32 = jnp.int32

NP = 50
NQ = 25
OW = 4
NO = 64
PAIRS = ((0, 1), (0, 2), (0, 3), (1, 2), (1, 3), (2, 3))
SLOT = 64
MSG = len(PAIRS) * SLOT
ZN = 8
YH = 2


def iota(shape, dim):
    return lax.broadcasted_iota(I32, shape, dim)


def dot(a, b, dims):
    return lax.dot_general(a, b, (dims, ((), ())), preferred_element_type=F32)


class Plan:
    def __init__(self, lanes, cap):
        self.lanes, self.cap = lanes, cap
        self.group = 128 // cap
        self.full = NQ // self.group
        self.wide = self.group * lanes // 128
        self.last = -(-lanes // 128)
        self.span = self.full * self.wide + self.last
        self.rest = -(-2 * (self.full + 1) // 16)
        self.count = 3 * self.span + self.rest * self.wide
        self.depth = (self.full + 1) * 128


NN = ((1,), (0,))
NT = ((1,), (1,))
TN = ((0,), (0,))


def kernel(plan, amps, integral, occ_row, occ, virt, out, blk, wblk, rest32, st, sw, ex, y32, texp, wall, c32, keep, psend,
           precv, msg, p2r, zmat, tile, p3r, ag_s, ag_r, w_s, w_r, d_s, d_r, p2_s, p2_rs, p3_s, p3_rs, word):
    group, wide, span, full = plan.group, plan.wide, plan.span, plan.full
    dense = plan.lanes == OW * NO
    row = lax.axis_index("row")
    col = lax.axis_index("col")
    core = row % 2
    chip = row // 2
    yh = col // ZN
    z = col % ZN

    right = yh * ZN + (z + 1) % ZN
    left = yh * ZN + (z + ZN - 1) % ZN
    opposite = (1 - yh) * ZN + z
    mate = row + 1 - 2 * core
    home = chip // ZN
    home_z = chip % ZN
    late_owner = home_z == (z + 4) % ZN
    mirror_col = row // 2
    own_p2 = (home == yh).astype(I32)
    own_p3 = (mirror_col == col).astype(I32)

    x, y = row // 8, yh * 4 + chip % 4

    def at_x(d):
        return ((x + 4 + d) % 4 * 8 + row % 8, col)

    def at_y(d):
        to = (y + 8 + d) % 8
        return (x * 8 + to % 4 * 2 + core, to // 4 * ZN + z)

    def at_z(d):
        return (row, yh * ZN + (z + ZN + d) % ZN)

    bar = pltpu.get_barrier_semaphore()
    near = [at(d) for at in (at_x, at_y, at_z) for d in (1, -1)] + [(mate, col)]
    for to in near:
        pl.semaphore_signal(bar, inc=1, device_id=to, device_id_type=MESH)

    rounds = ((at_y, 2), (at_y, 2), (at_y, 1), (at_x, 2), (at_x, 1), (None, 1), (at_z, 2), (at_z, 2), (at_z, 2), (at_z, 1))

    def tell(n):
        at, ways = rounds[n]
        for way in range(ways):
            to = (mate, col) if at is None else at(1 - 2 * way)
            pl.semaphore_signal(word.at[2 * n + way], inc=1, device_id=to, device_id_type=MESH)

    def hear(n):
        for way in range(rounds[n][1]):
            pl.semaphore_wait(word.at[2 * n + way], 1)

    block_irrep = virt[row // 4]
    lab = occ_row[...]

    def offsets(label):
        counts = [jnp.sum(jnp.where(lab == (label ^ occ[i]), 1.0, 0.0), axis=1, keepdims=True).astype(I32) for i in range(OW)]
        if dense:
            return [jnp.full((1, 1), i * NO, I32) for i in range(OW)], [jnp.full((1, 1), NO, I32)] * OW
        return [sum(counts[:i], jnp.zeros((1, 1), I32)) for i in range(OW)], counts

    def by_window(which, values):
        return jnp.where(which == 0, values[0], jnp.where(which == 1, values[1], jnp.where(which == 2, values[2], values[3])))

    labf = lab.astype(F32)
    r256, l64 = iota((256, NO), 0), iota((256, NO), 1)
    here = virt[col // 2] ^ block_irrep
    here_off, _ = offsets(here)
    pl_lane = iota((1, group * plan.lanes), 1)

    def select(ref, k_of, i_of):
        hk = jnp.sum(jnp.where(l64 == k_of, labf, 0.0), axis=1, keepdims=True)
        k1, i1 = k_of[:, :1], i_of[:, :1]
        hi = by_window(i1, [occ[i] for i in range(OW)])
        if dense:
            place = k1
        else:
            same = (labf == hk) & (l64 < k_of)
            place = jnp.sum(jnp.where(same, 1.0, 0.0), axis=1, keepdims=True).astype(I32)
        key = jnp.where((hk.astype(I32) ^ hi) == here, by_window(i1, here_off) + place, -1)
        for g in range(group):
            hit = (key == pl_lane % plan.lanes) & (pl_lane // plan.lanes == g)
            ref[g * 256:(g + 1) * 256, :] = jnp.where(hit, 1.0, 0.0).astype(BF16)

    def pack(planes, sel, dst):
        for q in range(full + 1):
            cs = range(q * group, min(NQ, (q + 1) * group))
            many = wide if q < full else plan.last
            x = jnp.concatenate([planes[c] for c in cs], axis=1)
            y = dot(x, sel[0:len(cs) * 256, 0:many * 128], NN)
            for r in range(3):
                for t in range(many):
                    dst[r * span + q * wide + t] = y[r * 16:(r + 1) * 16, t * 128:(t + 1) * 128].astype(BF16)
            rest32[2 * q:2 * q + 2, 0:many * 128] = y[48:50, :]
        for r in range(plan.rest):
            for t in range(wide):
                dst[3 * span + r * wide + t] = rest32[r * 16:(r + 1) * 16, t * 128:(t + 1) * 128].astype(BF16)

    def expand(src, sel, dst):
        lines = [jnp.concatenate([src[r * span + q * wide + t] for t in range(wide)], axis=1)
                 for q in range(full) for r in range(3)]
        lines += [jnp.concatenate([src[3 * span + r * wide + t] for t in range(wide)], axis=1) for r in range(plan.rest)]
        tall = 48 * full
        y32[0:tall + 16 * plan.rest, :] = dot(jnp.concatenate(lines, axis=0), sel[...], NN)
        x = jnp.concatenate([jnp.concatenate([src[r * span + full * wide + t] for t in range(plan.last)], axis=1)
                             for r in range(3)], axis=0)
        z6 = dot(x, sel[0:plan.last * 128, :], NN)
        for q in range(full + 1):
            for i in range(OW):
                lanes = slice(i * 128, (i + 1) * 128)
                main = y32[q * 48:(q + 1) * 48, lanes] if q < full else z6[:, lanes]
                dst[i * SLOT:i * SLOT + 48, q * 128:(q + 1) * 128] = main.astype(BF16)
                dst[i * SLOT + 48:i * SLOT + 50, q * 128:(q + 1) * 128] = (
                    y32[tall + 2 * q:tall + 2 * q + 2, lanes].astype(BF16))

    rest32[...] = jnp.zeros(rest32.shape, F32)
    select(st, r256 % NO, r256 // NO)
    pack(amps, st, blk.at[z])

    pl.semaphore_wait(bar, len(near))

    cut = plan.count // 2
    parts = ((0, cut), (cut, plan.count - cut))

    def moved(direction, step, part, src):
        lo, size = parts[part]
        n = (direction * 4 + step) * 2 + part
        ref = blk.at[src, pl.ds(lo, size)]
        return pltpu.make_async_remote_copy(
            src_ref=ref, dst_ref=ref, send_sem=ag_s.at[n], recv_sem=ag_r.at[n],
            device_id=(row, right if direction == 0 else left), device_id_type=MESH)

    def hop(direction, step, part):
        return moved(direction, step, part, (z + ZN - step) % ZN if direction == 0 else (z + step) % ZN)

    def arrival(direction, step, part):
        return moved(direction, step, part, (z + ZN - step - 1) % ZN if direction == 0 else (z + step + 1) % ZN)

    for part in range(2):
        for d in range(2):
            hop(d, 0, part).start()

    tell(0)
    select(sw, r256 // OW, r256 % OW)
    hear(0)
    tell(1)
    pack(integral, sw, wblk.at[yh])
    hear(1)
    tell(2)

    def swap(which):
        return pltpu.make_async_remote_copy(
            src_ref=wblk.at[which], dst_ref=wblk.at[which], send_sem=w_s, recv_sem=w_r, device_id=(row, opposite),
            device_id_type=MESH)

    er = iota((group * plan.lanes, 1), 0)
    el = iota((1, 512), 1)
    e_i, e_g, e_m = el // 128, (el % 128) // plan.cap, el % plan.cap
    for n in range(5):
        label = block_irrep ^ (virt[yh * 4 + n] if n < 4 else virt[(1 - yh) * 4 + z // 2])
        off, counts = offsets(label)
        key = jnp.where(e_m < by_window(e_i, counts), by_window(e_i, off) + e_m, -1)
        hit = (er % plan.lanes == key) & (er // plan.lanes == e_g)
        ex[n] = jnp.where(hit, 1.0, 0.0).astype(BF16)

    hear(2)
    swap(yh).start()
    tell(3)
    texp[...] = jnp.zeros(texp.shape, BF16)
    wall[...] = jnp.zeros(wall.shape, BF16)
    hear(3)
    tell(4)

    zr, zl = iota((MSG, OW * 256), 0), iota((MSG, OW * 256), 1)
    zp, zb = zr // SLOT, zr % SLOT
    zi, zt = zl // 256, zl % 256
    first = jnp.where(zp < 3, 0, jnp.where(zp < 5, 1, 2))
    second = jnp.where(zp < 3, zp + 1, jnp.where(zp < 5, zp - 1, 3))
    in_b = (zt // OW == zb) & (zb < NP)
    plus = in_b & (zi == first) & (zt % OW == second)
    minus = in_b & (zi == second) & (zt % OW == first)
    zmat[...] = (jnp.where(plus, 1.0, 0.0) - jnp.where(minus, 1.0, 0.0)).astype(BF16)

    low = iota((32, 128), 1) < SLOT
    order = (0, ZN - 1, 1, ZN - 2, 2, ZN - 3, 3, 4)

    def unpack(n):
        za = (z + order[n]) % ZN
        expand(blk.at[za], ex.at[za // 2], texp.at[n])

    def mate_copy(n):
        return pltpu.make_async_remote_copy(
            src_ref=psend.at[n], dst_ref=precv.at[n], send_sem=d_s.at[n], recv_sem=d_r.at[n], device_id=(mate, col),
            device_id_type=MESH)

    def differences(n):
        za = (z + order[n]) % ZN
        for h in range(YH):
            c32[:, h * 256:(h + 1) * 256] = dot(texp[n], wall[h], NT)
        la = virt[(yh * ZN + za) // 2]
        halves = []
        for half in range(2):
            line = []
            for h in range(YH):
                lb = virt[(h * ZN + z) // 2]
                for t in range(3):
                    both = []
                    for p in (2 * t, 2 * t + 1):
                        i, j = PAIRS[p]

                        def piece(r, s):
                            start = SLOT * r + NQ * half
                            v = c32[start:start + 32, h * 256 + (s // 2) * 128:h * 256 + (s // 2) * 128 + 128]
                            return v if s % 2 == p % 2 else pltpu.roll(v, SLOT, axis=1)

                        scale = jnp.where((la ^ lb ^ occ[i] ^ occ[j]) == 0, 1.0, 0.0)
                        both.append((piece(i, j) - piece(j, i)) * scale)
                    line.append(jnp.where(low, both[0], both[1]))
            halves.append(jnp.concatenate(line, axis=1))
        return halves

    def compute(n):
        halves = differences(n)
        keep[n] = jnp.where(core == 0, halves[0], halves[1])
        psend[n] = jnp.where(core == 0, halves[1], halves[0]).astype(BF16)
        mate_copy(n).start()

    def deliver(m, to_row, h, place):
        mine = (to_row == row) & (yh == h)

        @pl.when(jnp.logical_not(mine))
        def _():
            pltpu.make_async_remote_copy(
                src_ref=msg.at[m], dst_ref=p2r.at[place], send_sem=p2_s, recv_sem=p2_rs,
                device_id=(to_row, h * ZN + z), device_id_type=MESH).start()

        @pl.when(mine)
        def _():
            pltpu.make_async_copy(msg.at[m], p2r.at[place], p2_rs).start()

    def finish(n):
        za = (z + order[n]) % ZN
        mate_copy(n).wait_recv()
        total = (keep[n] + precv[n].astype(F32)).astype(BF16)
        for h in range(YH):
            msg[2 * n + h] = total[:, h * MSG:(h + 1) * MSG]
            deliver(2 * n + h, 2 * (yh * ZN + za) + core, h, chip)

    def forward(step):
        for part in range(2):
            for d in range(2):
                arrival(d, step - 1, part).wait_recv()
                if step < 3 or part == d:
                    hop(d, step, part).start()

    hear(4)
    tell(5)
    expand(wblk.at[yh], ex.at[z // 2], wall.at[yh])
    unpack(0)
    hear(5)
    tell(6)
    forward(1)
    unpack(1)
    unpack(2)
    hear(6)
    tell(7)
    forward(2)
    unpack(3)
    unpack(4)
    hear(7)
    tell(8)
    swap(1 - yh).wait_recv()
    expand(wblk.at[1 - yh], ex.at[4], wall.at[1 - yh])
    compute(0)
    forward(3)
    hear(8)
    tell(9)
    for n in range(1, 5):
        compute(n)
    for n in (5, 6):
        unpack(n)
        compute(n)
    for n in range(7):
        finish(n)
    for d in range(2):
        arrival(d, 3, d).wait_recv()
    unpack(7)
    halves = differences(7)
    za = (z + order[7]) % ZN
    for half in range(2):
        total = halves[half].astype(BF16)
        for h in range(YH):
            m = 14 + 2 * half + h
            msg[m] = total[:, h * MSG:(h + 1) * MSG]
            deliver(m, 2 * (yh * ZN + za) + half, h, row)

    def add_up(many):
        pltpu.make_async_copy(p2r.at[pl.ds(0, many)], p2r.at[pl.ds(0, many)], p2_rs).wait()
        total = p2r[0].astype(F32)
        for n in range(1, many):
            total = total + p2r[n].astype(F32)
        tile[...] = total.astype(BF16)

    @pl.when(late_owner)
    def _():
        add_up(32)

    @pl.when(jnp.logical_not(late_owner))
    def _():
        add_up(16)

    hear(9)
    def mirror_copy(s):
        return pltpu.make_async_remote_copy(
            src_ref=tile, dst_ref=p3r.at[row % 2], send_sem=p3_s.at[s], recv_sem=p3_rs.at[row % 2],
            device_id=(2 * col + s, mirror_col), device_id_type=MESH)

    for s in range(2):
        self_mirror = (2 * col + s == row) & (mirror_col == col)

        @pl.when(jnp.logical_not(self_mirror))
        def _():
            mirror_copy(s).start()

        @pl.when(self_mirror)
        def _():
            pltpu.make_async_copy(tile, p3r.at[s], p3_rs.at[s]).start()

    base = dot(tile[...], zmat[...], NN)
    br, bl = iota((32, 256), 0), iota((32, 256), 1)
    spread = None
    for s in range(2):
        pltpu.make_async_copy(p3r.at[s], p3r.at[s], p3_rs.at[s]).wait()
        put = ((bl % 128) == br + NQ * s + SLOT * (bl // 128)) & (br < NQ)
        part = dot(p3r[s], jnp.where(put, 1.0, 0.0).astype(BF16), TN)
        spread = part if spread is None else spread + part
    line = []
    for t in range(3):
        both = []
        for u in range(2):
            lo = (2 * t + u) * SLOT
            a0 = spread[lo:lo + 32, u * 128:(u + 1) * 128]
            a1 = spread[lo + NQ:lo + NQ + 32, u * 128:(u + 1) * 128]
            both.append(jnp.where(row % 2 == 0, a0, a1))
        line.append(both[0] + both[1])
    swapped = jnp.concatenate(line, axis=1).astype(BF16)
    res = base - dot(swapped, zmat[...], NN)
    for i in range(OW):
        out[i] = res[0:NQ, i * 256:i * 256 + NP * OW]

    for part in range(2):
        for d in range(2):
            for step in range(4):
                if step < 3 or part == d:
                    hop(d, step, part).wait_send()
    swap(yh).wait_send()
    for n in range(7):
        mate_copy(n).wait_send()

    @pl.when(home == yh)
    def _():
        pltpu.make_async_copy(msg.at[pl.ds(0, 17)], msg.at[pl.ds(0, 17)], p2_s).wait()

    @pl.when(home != yh)
    def _():
        pltpu.make_async_copy(msg, msg, p2_s).wait()

    for s in range(2):
        @pl.when(jnp.logical_not((2 * col + s == row) & (mirror_col == col)))
        def _():
            mirror_copy(s).wait_send()


def call(lanes, cap, collective_id, amps, integral, virt_irrep, occ_irrep):
    plan = Plan(lanes, cap)
    vmem = pl.BlockSpec(memory_space=pltpu.VMEM)
    smem = pl.BlockSpec(memory_space=pltpu.SMEM)
    dma = pltpu.SemaphoreType.DMA
    return pl.pallas_call(
        functools.partial(kernel, plan),
        out_shape=jax.ShapeDtypeStruct((OW, NQ, NP * OW), F32),
        in_specs=[vmem, vmem, vmem, smem, smem],
        out_specs=vmem,
        scratch_shapes=[
            pltpu.VMEM((ZN, plan.count, 16, 128), BF16),
            pltpu.VMEM((YH, plan.count, 16, 128), BF16),
            pltpu.VMEM((plan.rest * 16, plan.wide * 128), F32),
            pltpu.VMEM((plan.group * 256, plan.wide * 128), BF16),
            pltpu.VMEM((plan.group * 256, plan.wide * 128), BF16),
            pltpu.VMEM((5, plan.wide * 128, 512), BF16),
            pltpu.VMEM((48 * plan.full + 16 * plan.rest, 512), F32),
            pltpu.VMEM((ZN, OW * SLOT, plan.depth), BF16),
            pltpu.VMEM((YH, OW * SLOT, plan.depth), BF16),
            pltpu.VMEM((OW * SLOT, 512), F32),
            pltpu.VMEM((ZN - 1, 32, YH * MSG), F32),
            pltpu.VMEM((ZN - 1, 32, YH * MSG), BF16),
            pltpu.VMEM((ZN - 1, 32, YH * MSG), BF16),
            pltpu.VMEM((18, 32, MSG), BF16),
            pltpu.VMEM((32, 32, MSG), BF16),
            pltpu.VMEM((MSG, OW * 256), BF16),
            pltpu.VMEM((32, MSG), BF16),
            pltpu.VMEM((2, 32, MSG), BF16),
            dma((16,)), dma((16,)), dma, dma, dma((ZN - 1,)), dma((ZN - 1,)), dma, dma, dma((2,)), dma((2,)),
            pltpu.SemaphoreType.REGULAR((20,)),
        ],
        name="cycle%d" % lanes,
        compiler_params=pltpu.CompilerParams(
            collective_id=collective_id, has_side_effects=True, vmem_limit_bytes=48 * 2**20),
    )(amps, integral, occ_irrep.reshape(1, NO), occ_irrep, virt_irrep)


TIERS = ((64, 32), (96, 32), (OW * NO, NO))


def shards(amps, integral, virt_irrep, occ_irrep):
    partner = jnp.concatenate([occ_irrep[:OW], jnp.zeros((1,), I32)])
    weight = jnp.array([1, 1, 1, 1, 1024], I32)
    hits = (occ_irrep[:, None, None] ^ partner[None, :, None]) == jnp.arange(8, dtype=I32)
    sums = jnp.sum(jnp.where(hits, weight[None, :, None], 0), axis=(0, 1))
    need = sums % 1024
    tier = jnp.max(jnp.where(sums // 1024 > 32, 2, (need > 64).astype(I32) + (need > 96).astype(I32)))
    calls = [functools.partial(call, lanes, cap, n) for n, (lanes, cap) in enumerate(TIERS)]
    tile = lax.switch(tier, calls, amps.transpose(1, 0, 2), integral, virt_irrep, occ_irrep)
    return tile.transpose(1, 0, 2)


def solution(mesh):
    placed = (P("col", "row", None), P("row", "col", None), P(), P())
    return jax.shard_map(
        shards, mesh=mesh, in_specs=placed, out_specs=P("row", None, "col"), check_vma=False
    )
```

time: 92.9 us -> 63.1 us (0.68)
  Pallas kernels: 90.7 us -> 59 us
  other arithmetic: 0 us -> 0.97 us
    pallas_call x1, Pallas kernels: 90.7 us -> 59 us  [call(): pl.pallas_call(functools.partial(kernel, plan), out_shape=jax.ShapeDtypeS...]
where the time goes in v2:
time: 63.1 us; the launch traced here: 62.9 us
  Pallas kernels  59 us (94%)
  local copies, waits for them, and re-layouts  1.96 us (3%)
  other arithmetic  0.97 us (2%)
  between operations  0.67 us (1%)
    pallas_call x1, Pallas kernels, call(): pl.pallas_call(functools.partial(kernel, plan), out_shape=jax.ShapeDtypeS...  59 us

profile of v2, /device:TPU:7, one launch (start us, length us, event | category | flops | bytes accessed | tf_op | source)
XLA Modules:
  0.0 62.9 jit_solution(17990809373307624553)
XLA Ops:
  0.0 0.0 copy-start
  0.0 0.7 %copy-done = s32[64]{0:T(128)S(1)} copy-done((s32[64]{0:T(128)S(1)}, s32[64]{0:T(128)}, u32[]{:S(2)}) %copy-start) | copy-done | bytes 280
  0.7 0.1 pad_add_fusion
  0.7 0.0 copy-start.2
  0.7 0.1 broadcast_xor_fusion
  0.8 0.6 copy-done.2
  1.4 0.2 select_reduce_fusion
  1.6 0.0 copy-start.1
  1.6 0.6 %fusion = s32[]{:T(128)} fusion(s32[8]{0:T(128)S(1)} %select_reduce_fusion), kind=kLoop, calls=%fused_computation.12 | loop fusion | flops 215 | bytes 36 | tf_op jit(solution)/shard_map/reduce_max | solution.py:471
  2.2 0.0 copy-done.1
  2.9 59.3 %conditional.1 = (f32[4,25,200]{2,1,0:T(8,128)S(1)}) conditional(s32[]{:T(128)} %clamp.3, (s32[64]{0:T(128)S(1)}, bf16[25,50,256]{2,1,0:T(8,128)(2,1)}, bf16[25,50,256]{2,1,0:T(8,128)(2,1)}, s32[8]{0:T(128)S(1)}) %tuple.24, (s32[64]{0:T(128)S(1)}, bf16[25,50,256]{2,1,0:T(8,128)(2,1)}, bf16[25,50,256]{2,1,0:T(8,128)(2,1)}, ...), branch_computations={%region_2.3_spmd, %region_3.4_spmd, %region_4.5_spmd} | conditional | bytes 8 | solution.py:473
  2.9 59.0 %cycle64.1 = f32[4,25,200]{2,1,0:T(8,128)S(1)} custom-call(bf16[25,50,256]{2,1,0:T(8,128)(2,1)} %get-tuple-element.32.amps, bf16[25,50,256]{2,1,0:T(8,128)(2,1)} %get-tuple-element.34.integral, s32[1,64]{1,0:T(1,128)S(1)} %bitcast.12, s32[64]{0:T(128)S(1)} %get-tuple-element.35.occ, s32[8]{0:T(128)S(1)} %get-tuple-element.36.virt), custom_call_target="tpu_custom_call" | custom-call | tf_op jit(solution)/shard_map/cond/branch_0_fun/cycle64/pallas_call | solution.py:429
  62.2 0.7 %copy.9 = f32[4,25,200]{2,0,1:T(4,128)} copy(f32[4,25,200]{2,1,0:T(8,128)S(1)} %get-tuple-element.45) | data formatting | bytes 160000 | tf_op jit(solution)/shard_map/cond | solution.py:473
Async XLA Ops:
  0.0 0.7 %copy-start = (s32[64]{0:T(128)S(1)}, s32[64]{0:T(128)}, u32[]{:S(2)}) copy-start(s32[64]{0:T(128)} %param.11) | copy-start | bytes 772
  0.7 0.7 %copy-start.2 = (s32[5]{0:T(128)S(1)}, s32[5]{0:T(128)}, u32[]{:S(2)}) copy-start(s32[5]{0:T(128)} %constant.43.clone) | copy-start | bytes 64
  1.6 0.7 %copy-start.1 = (s32[8]{0:T(128)S(1)}, s32[8]{0:T(128)}, u32[]{:S(2)}) copy-start(s32[8]{0:T(128)} %param.10) | copy-start | bytes 100

commit v3 on v2

--- a/solution.py
+++ b/solution.py
@@ -2,6 +2,7 @@
 
 import jax
 import jax.numpy as jnp
+import numpy as np
 from jax import lax
 from jax.experimental import pallas as pl
 from jax.experimental.pallas import tpu as pltpu
@@ -18,7 +19,6 @@
 NO = 64
 PAIRS = ((0, 1), (0, 2), (0, 3), (1, 2), (1, 3), (2, 3))
 SLOT = 64
-MSG = len(PAIRS) * SLOT
 ZN = 8
 YH = 2
 
@@ -32,8 +32,9 @@
 
 
 class Plan:
-    def __init__(self, lanes, cap):
-        self.lanes, self.cap = lanes, cap
+    def __init__(self, lanes, cap, slots):
+        self.lanes, self.cap, self.slots = lanes, cap, slots
+        self.msg = slots * SLOT
         self.group = 128 // cap
         self.full = NQ // self.group
         self.wide = self.group * lanes // 128
@@ -88,17 +89,18 @@
     for to in near:
         pl.semaphore_signal(bar, inc=1, device_id=to, device_id_type=MESH)
 
-    rounds = ((at_y, 2), (at_y, 2), (at_y, 1), (at_x, 2), (at_x, 1), (None, 1), (at_z, 2), (at_z, 2), (at_z, 2), (at_z, 1))
+    rounds = (
+        ((at_y, 1), (at_y, -1)), ((at_x, 1), (at_x, -1), (at_y, 2), (at_y, -2)), ((at_y, 3), (at_y, -3)),
+        (None,), ((at_z, 1), (at_z, -1)), ((at_z, 2), (at_z, -2)), ((at_z, 1),))
 
     def tell(n):
-        at, ways = rounds[n]
-        for way in range(ways):
-            to = (mate, col) if at is None else at(1 - 2 * way)
-            pl.semaphore_signal(word.at[2 * n + way], inc=1, device_id=to, device_id_type=MESH)
+        for way, to in enumerate(rounds[n]):
+            pl.semaphore_signal(word.at[4 * n + way], inc=1, device_id=(mate, col) if to is None else to[0](to[1]),
+                                device_id_type=MESH)
 
     def hear(n):
-        for way in range(rounds[n][1]):
-            pl.semaphore_wait(word.at[2 * n + way], 1)
+        for way in range(len(rounds[n])):
+            pl.semaphore_wait(word.at[4 * n + way], 1)
 
     block_irrep = virt[row // 4]
     lab = occ_row[...]
@@ -192,11 +194,9 @@
 
     tell(0)
     select(sw, r256 // OW, r256 % OW)
+    pack(integral, sw, wblk.at[yh])
     hear(0)
     tell(1)
-    pack(integral, sw, wblk.at[yh])
-    hear(1)
-    tell(2)
 
     def swap(which):
         return pltpu.make_async_remote_copy(
@@ -213,23 +213,30 @@
         hit = (er % plan.lanes == key) & (er // plan.lanes == e_g)
         ex[n] = jnp.where(hit, 1.0, 0.0).astype(BF16)
 
-    hear(2)
-    swap(yh).start()
-    tell(3)
-    texp[...] = jnp.zeros(texp.shape, BF16)
-    wall[...] = jnp.zeros(wall.shape, BF16)
-    hear(3)
-    tell(4)
-
-    zr, zl = iota((MSG, OW * 256), 0), iota((MSG, OW * 256), 1)
-    zp, zb = zr // SLOT, zr % SLOT
-    zi, zt = zl // 256, zl % 256
-    first = jnp.where(zp < 3, 0, jnp.where(zp < 5, 1, 2))
-    second = jnp.where(zp < 3, zp + 1, jnp.where(zp < 5, zp - 1, 3))
-    in_b = (zt // OW == zb) & (zb < NP)
-    plus = in_b & (zi == first) & (zt % OW == second)
-    minus = in_b & (zi == second) & (zt % OW == first)
-    zmat[...] = (jnp.where(plus, 1.0, 0.0) - jnp.where(minus, 1.0, 0.0)).astype(BF16)
+    def slots(label):
+        alive = [(occ[i] ^ occ[j]) == label for i, j in PAIRS]
+        if plan.slots == len(PAIRS):
+            return [[alive[p] if p == n else None for p in range(len(PAIRS))] for n in range(plan.slots)]
+        ones = [jnp.where(a, 1, 0) for a in alive]
+        return [[alive[p] & (sum(ones[:p], 0) == n) if p >= n else None for p in range(len(PAIRS))]
+                for n in range(plan.slots)]
+
+    def spread_matrix():
+        zr, zl = iota((plan.msg, OW * 256), 0), iota((plan.msg, OW * 256), 1)
+        zr1 = zr[:, :1]
+        first = second = jnp.full((plan.msg, 1), -1, I32)
+        for n, taken in enumerate(slots(here)):
+            for p, (i, j) in enumerate(PAIRS):
+                if taken[p] is not None:
+                    it = (zr1 // SLOT == n) & taken[p]
+                    first, second = jnp.where(it, i, first), jnp.where(it, j, second)
+        zb = zr1 % SLOT
+        zl1 = zl[:1]
+        zi, zt = zl1 // 256, zl1 % 256
+        in_b = (zt // OW == zb) & (zb < NP)
+        plus = in_b & (zi == first) & (zt % OW == second)
+        minus = in_b & (zi == second) & (zt % OW == first)
+        zmat[...] = (jnp.where(plus, 1.0, 0.0) - jnp.where(minus, 1.0, 0.0)).astype(BF16)
 
     low = iota((32, 128), 1) < SLOT
     order = (0, ZN - 1, 1, ZN - 2, 2, ZN - 3, 3, 4)
@@ -248,24 +255,26 @@
         for h in range(YH):
             c32[:, h * 256:(h + 1) * 256] = dot(texp[n], wall[h], NT)
         la = virt[(yh * ZN + za) // 2]
+        taken_by = [slots(la ^ virt[(h * ZN + z) // 2]) for h in range(YH)]
         halves = []
         for half in range(2):
             line = []
             for h in range(YH):
-                lb = virt[(h * ZN + z) // 2]
-                for t in range(3):
-                    both = []
-                    for p in (2 * t, 2 * t + 1):
-                        i, j = PAIRS[p]
-
-                        def piece(r, s):
-                            start = SLOT * r + NQ * half
-                            v = c32[start:start + 32, h * 256 + (s // 2) * 128:h * 256 + (s // 2) * 128 + 128]
-                            return v if s % 2 == p % 2 else pltpu.roll(v, SLOT, axis=1)
-
-                        scale = jnp.where((la ^ lb ^ occ[i] ^ occ[j]) == 0, 1.0, 0.0)
-                        both.append((piece(i, j) - piece(j, i)) * scale)
-                    line.append(jnp.where(low, both[0], both[1]))
+                values = []
+                for i, j in PAIRS:
+
+                    def piece(r, q):
+                        start = SLOT * r + NQ * half
+                        v = c32[start:start + 32, h * 256 + (q // 2) * 128:h * 256 + (q // 2) * 128 + 128]
+                        return v if q % 2 == 0 else pltpu.roll(v, SLOT, axis=1)
+
+                    values.append(piece(i, j) - piece(j, i))
+                pieces = []
+                for n, taken in enumerate(taken_by[h]):
+                    v = sum(values[p] * jnp.where(t, 1.0, 0.0) for p, t in enumerate(taken) if t is not None)
+                    pieces.append(v if n % 2 == 0 else pltpu.roll(v, SLOT, axis=1))
+                for n in range(0, plan.slots, 2):
+                    line.append(jnp.where(low, pieces[n], pieces[n + 1]))
             halves.append(jnp.concatenate(line, axis=1))
         return halves
 
@@ -293,7 +302,7 @@
         mate_copy(n).wait_recv()
         total = (keep[n] + precv[n].astype(F32)).astype(BF16)
         for h in range(YH):
-            msg[2 * n + h] = total[:, h * MSG:(h + 1) * MSG]
+            msg[2 * n + h] = total[:, h * plan.msg:(h + 1) * plan.msg]
             deliver(2 * n + h, 2 * (yh * ZN + za) + core, h, chip)
 
     def forward(step):
@@ -303,35 +312,40 @@
                 if step < 3 or part == d:
                     hop(d, step, part).start()
 
-    hear(4)
-    tell(5)
+    hear(1)
+    swap(yh).start()
+    tell(2)
+    forward(1)
+    texp[...] = jnp.zeros(texp.shape, BF16)
+    wall[...] = jnp.zeros(wall.shape, BF16)
     expand(wblk.at[yh], ex.at[z // 2], wall.at[yh])
     unpack(0)
-    hear(5)
-    tell(6)
-    forward(1)
+    hear(2)
+    tell(3)
     unpack(1)
     unpack(2)
-    hear(6)
-    tell(7)
     forward(2)
+    hear(3)
+    tell(4)
+    spread_matrix()
     unpack(3)
     unpack(4)
-    hear(7)
-    tell(8)
     swap(1 - yh).wait_recv()
     expand(wblk.at[1 - yh], ex.at[4], wall.at[1 - yh])
     compute(0)
+    compute(1)
     forward(3)
-    hear(8)
-    tell(9)
-    for n in range(1, 5):
+    hear(4)
+    tell(5)
+    for n in range(2, 7):
+        if n > 4:
+            unpack(n)
         compute(n)
-    for n in (5, 6):
-        unpack(n)
-        compute(n)
-    for n in range(7):
-        finish(n)
+        finish(n - 2)
+    hear(5)
+    tell(6)
+    finish(5)
+    finish(6)
     for d in range(2):
         arrival(d, 3, d).wait_recv()
     unpack(7)
@@ -341,7 +355,7 @@
         total = halves[half].astype(BF16)
         for h in range(YH):
             m = 14 + 2 * half + h
-            msg[m] = total[:, h * MSG:(h + 1) * MSG]
+            msg[m] = total[:, h * plan.msg:(h + 1) * plan.msg]
             deliver(m, 2 * (yh * ZN + za) + half, h, row)
 
     def add_up(many):
@@ -359,7 +373,7 @@
     def _():
         add_up(16)
 
-    hear(9)
+    hear(6)
     def mirror_copy(s):
         return pltpu.make_async_remote_copy(
             src_ref=tile, dst_ref=p3r.at[row % 2], send_sem=p3_s.at[s], recv_sem=p3_rs.at[row % 2],
@@ -385,7 +399,7 @@
         part = dot(p3r[s], jnp.where(put, 1.0, 0.0).astype(BF16), TN)
         spread = part if spread is None else spread + part
     line = []
-    for t in range(3):
+    for t in range(plan.slots // 2):
         both = []
         for u in range(2):
             lo = (2 * t + u) * SLOT
@@ -421,8 +435,8 @@
             mirror_copy(s).wait_send()
 
 
-def call(lanes, cap, collective_id, amps, integral, virt_irrep, occ_irrep):
-    plan = Plan(lanes, cap)
+def call(lanes, cap, slots, collective_id, amps, integral, virt_irrep, occ_irrep):
+    plan = Plan(lanes, cap, slots)
     vmem = pl.BlockSpec(memory_space=pltpu.VMEM)
     smem = pl.BlockSpec(memory_space=pltpu.SMEM)
     dma = pltpu.SemaphoreType.DMA
@@ -442,16 +456,16 @@
             pltpu.VMEM((ZN, OW * SLOT, plan.depth), BF16),
             pltpu.VMEM((YH, OW * SLOT, plan.depth), BF16),
             pltpu.VMEM((OW * SLOT, 512), F32),
-            pltpu.VMEM((ZN - 1, 32, YH * MSG), F32),
-            pltpu.VMEM((ZN - 1, 32, YH * MSG), BF16),
-            pltpu.VMEM((ZN - 1, 32, YH * MSG), BF16),
-            pltpu.VMEM((18, 32, MSG), BF16),
-            pltpu.VMEM((32, 32, MSG), BF16),
-            pltpu.VMEM((MSG, OW * 256), BF16),
-            pltpu.VMEM((32, MSG), BF16),
-            pltpu.VMEM((2, 32, MSG), BF16),
+            pltpu.VMEM((ZN - 1, 32, YH * plan.msg), F32),
+            pltpu.VMEM((ZN - 1, 32, YH * plan.msg), BF16),
+            pltpu.VMEM((ZN - 1, 32, YH * plan.msg), BF16),
+            pltpu.VMEM((18, 32, plan.msg), BF16),
+            pltpu.VMEM((32, 32, plan.msg), BF16),
+            pltpu.VMEM((plan.msg, OW * 256), BF16),
+            pltpu.VMEM((32, plan.msg), BF16),
+            pltpu.VMEM((2, 32, plan.msg), BF16),
             dma((16,)), dma((16,)), dma, dma, dma((ZN - 1,)), dma((ZN - 1,)), dma, dma, dma((2,)), dma((2,)),
-            pltpu.SemaphoreType.REGULAR((20,)),
+            pltpu.SemaphoreType.REGULAR((28,)),
         ],
         name="cycle%d" % lanes,
         compiler_params=pltpu.CompilerParams(
@@ -459,17 +473,25 @@
     )(amps, integral, occ_irrep.reshape(1, NO), occ_irrep, virt_irrep)
 
 
-TIERS = ((64, 32), (96, 32), (OW * NO, NO))
+TIERS = ((64, 32, 2), (96, 32, 4), (OW * NO, NO, 6))
 
 
 def shards(amps, integral, virt_irrep, occ_irrep):
     partner = jnp.concatenate([occ_irrep[:OW], jnp.zeros((1,), I32)])
-    weight = jnp.array([1, 1, 1, 1, 1024], I32)
-    hits = (occ_irrep[:, None, None] ^ partner[None, :, None]) == jnp.arange(8, dtype=I32)
-    sums = jnp.sum(jnp.where(hits, weight[None, :, None], 0), axis=(0, 1))
-    need = sums % 1024
-    tier = jnp.max(jnp.where(sums // 1024 > 32, 2, (need > 64).astype(I32) + (need > 96).astype(I32)))
-    calls = [functools.partial(call, lanes, cap, n) for n, (lanes, cap) in enumerate(TIERS)]
+    weight = np.full((NO, OW + 1, 1), 1, np.int32)
+    weight[:, OW] = 1 << 10
+    weight[:OW, :OW] += 1 << 18
+    irreps = jnp.arange(8, dtype=I32)
+    hits = (occ_irrep[:, None, None] ^ partner[None, :, None]) == irreps
+    sums = jnp.sum(jnp.where(hits, weight, 0), axis=(0, 1))
+    need = sums % (1 << 10)
+    most = (sums % (1 << 18)) // (1 << 10)
+    pairs = (sums // (1 << 18) - jnp.where(irreps == 0, OW, 0)) // 2
+    tier = jnp.zeros((8,), I32)
+    for lanes, cap, slots in TIERS[:-1]:
+        tier = tier + jnp.where((need > lanes) | (most > cap) | (pairs > slots), 1, 0)
+    tier = jnp.max(tier)
+    calls = [functools.partial(call, lanes, cap, slots, n) for n, (lanes, cap, slots) in enumerate(TIERS)]
     tile = lax.switch(tier, calls, amps.transpose(1, 0, 2), integral, virt_irrep, occ_irrep)
     return tile.transpose(1, 0, 2)
 

time: 63.1 us -> 59.4 us (0.941)
  Pallas kernels: 59 us -> 55.6 us
    pallas_call x1, Pallas kernels: 59 us -> 55.6 us  [call(): pl.pallas_call(functools.partial(kernel, plan), out_shape=jax.ShapeDtypeS...]
where the time goes in v3:
time: 59.4 us; the launch traced here: 59.2 us
  Pallas kernels  55.6 us (94%)
  local copies, waits for them, and re-layouts  1.37 us (2%)
  other arithmetic  0.92 us (2%)
  loops' own time  0.69 us (1%)
  between operations  0.67 us (1%)
    pallas_call x1, Pallas kernels, call(): pl.pallas_call(functools.partial(kernel, plan), out_shape=jax.ShapeDtypeS...  55.6 us

profile of v3, /device:TPU:7, one launch (start us, length us, event | category | flops | bytes accessed | tf_op | source)
XLA Modules:
  0.0 59.2 jit_solution(9684385720559712147)
XLA Ops:
  0.0 0.0 copy-start
  0.0 0.0 copy-start.2
  0.0 0.7 %copy-done = s32[64]{0:T(128)S(1)} copy-done((s32[64]{0:T(128)S(1)}, s32[64]{0:T(128)}, u32[]{:S(2)}) %copy-start) | copy-done | bytes 280
  0.7 0.1 pad_add_fusion
  0.7 0.1 broadcast_xor_fusion
  0.8 0.0 copy-done.2
  0.8 0.1 select_reduce_fusion
  0.9 0.0 copy-start.1
  0.9 0.7 %add_reduce_fusion = s32[]{:T(128)} fusion(s32[8]{0:T(128)S(1)} %select_reduce_fusion), kind=kLoop, calls=%fused_computation.24 | loop fusion | flops 583 | bytes 36 | tf_op jit(solution)/shard_map/reduce_max | solution.py:493
  1.6 0.0 copy-done.1
  2.2 56.2 %conditional.1 = (f32[4,25,200]{2,1,0:T(8,128)S(1)}) conditional(s32[]{:T(128)} %clamp.3, (s32[64]{0:T(128)S(1)}, bf16[25,50,256]{2,1,0:T(8,128)(2,1)}, bf16[25,50,256]{2,1,0:T(8,128)(2,1)}, s32[8]{0:T(128)S(1)}) %tuple.24, (s32[64]{0:T(128)S(1)}, bf16[25,50,256]{2,1,0:T(8,128)(2,1)}, bf16[25,50,256]{2,1,0:T(8,128)(2,1)}, ...), branch_computations={%region_2.3_spmd, %region_3.4_spmd, %region_4.5_spmd} | conditional | bytes 8 | solution.py:495
  2.4 55.6 %cycle96.1 = f32[4,25,200]{2,1,0:T(8,128)S(1)} custom-call(bf16[25,50,256]{2,1,0:T(8,128)(2,1)} %get-tuple-element.37.amps, bf16[25,50,256]{2,1,0:T(8,128)(2,1)} %get-tuple-element.38.integral, s32[1,64]{1,0:T(1,128)S(1)} %bitcast.13, s32[64]{0:T(128)S(1)} %get-tuple-element.39.occ, s32[8]{0:T(128)S(1)} %get-tuple-element.40.virt), custom_call_target="tpu_custom_call" | custom-call | tf_op jit(solution)/shard_map/cond/branch_1_fun/cycle96/pallas_call | solution.py:443
  58.5 0.7 %copy.9 = f32[4,25,200]{2,0,1:T(4,128)} copy(f32[4,25,200]{2,1,0:T(8,128)S(1)} %get-tuple-element.45) | data formatting | bytes 160000 | tf_op jit(solution)/shard_map/cond | solution.py:495
Async XLA Ops:
  0.0 0.7 %copy-start = (s32[64]{0:T(128)S(1)}, s32[64]{0:T(128)}, u32[]{:S(2)}) copy-start(s32[64]{0:T(128)} %param.11) | copy-start | bytes 772
  0.0 0.8 %copy-start.2 = (s32[64,5]{0,1:T(8,128)S(1)}, s32[64,5]{0,1:T(8,128)}, u32[]{:S(2)}) copy-start(s32[64,5]{0,1:T(8,128)} %constant.80) | copy-start | bytes 3844
  0.9 0.7 %copy-start.1 = (s32[8]{0:T(128)S(1)}, s32[8]{0:T(128)}, u32[]{:S(2)}) copy-start(s32[8]{0:T(128)} %param.10) | copy-start | bytes 100

commit v4 on v3

--- a/solution.py
+++ b/solution.py
@@ -35,6 +35,11 @@
     def __init__(self, lanes, cap, slots):
         self.lanes, self.cap, self.slots = lanes, cap, slots
         self.msg = slots * SLOT
+        self.parts = 2
+        self.near = 2 if slots == 2 else 3
+        self.paired = 2 * self.near - 1
+        self.messages = 2 * self.paired + 4 * (ZN - self.paired)
+        self.direct = slots == 2
         self.group = 128 // cap
         self.full = NQ // self.group
         self.wide = self.group * lanes // 128
@@ -51,7 +56,7 @@
 
 
 def kernel(plan, amps, integral, occ_row, occ, virt, out, blk, wblk, rest32, st, sw, ex, y32, texp, wall, c32, keep, psend,
-           precv, msg, p2r, zmat, tile, p3r, ag_s, ag_r, w_s, w_r, d_s, d_r, p2_s, p2_rs, p3_s, p3_rs, word):
+           precv, msg, p2r, zmat, tile, p3r, ag_s, ag_r, w_s, w_r, d_s, d_r, p2_s, p2_rs, p3_s, p3_rs, mir, m_s, m_rs, word):
     group, wide, span, full = plan.group, plan.wide, plan.span, plan.full
     dense = plan.lanes == OW * NO
     row = lax.axis_index("row")
@@ -67,10 +72,9 @@
     mate = row + 1 - 2 * core
     home = chip // ZN
     home_z = chip % ZN
-    late_owner = home_z == (z + 4) % ZN
+    gap = (home_z + ZN - z) % ZN
+    late_owner = (gap >= plan.near) & (gap <= ZN - plan.near)
     mirror_col = row // 2
-    own_p2 = (home == yh).astype(I32)
-    own_p3 = (mirror_col == col).astype(I32)
 
     x, y = row // 8, yh * 4 + chip % 4
 
@@ -171,13 +175,14 @@
 
     pl.semaphore_wait(bar, len(near))
 
-    cut = plan.count // 2
-    parts = ((0, cut), (cut, plan.count - cut))
+    edges = [plan.count * n // plan.parts for n in range(plan.parts + 1)]
+
+    def goes(direction, step, part):
+        return step < 3 or (part < plan.parts // 2) == (direction == 0)
 
     def moved(direction, step, part, src):
-        lo, size = parts[part]
-        n = (direction * 4 + step) * 2 + part
-        ref = blk.at[src, pl.ds(lo, size)]
+        n = (direction * 4 + step) * plan.parts + part
+        ref = blk.at[src, pl.ds(edges[part], edges[part + 1] - edges[part])]
         return pltpu.make_async_remote_copy(
             src_ref=ref, dst_ref=ref, send_sem=ag_s.at[n], recv_sem=ag_r.at[n],
             device_id=(row, right if direction == 0 else left), device_id_type=MESH)
@@ -188,7 +193,7 @@
     def arrival(direction, step, part):
         return moved(direction, step, part, (z + ZN - step - 1) % ZN if direction == 0 else (z + step + 1) % ZN)
 
-    for part in range(2):
+    for part in range(plan.parts):
         for d in range(2):
             hop(d, 0, part).start()
 
@@ -305,11 +310,33 @@
             msg[2 * n + h] = total[:, h * plan.msg:(h + 1) * plan.msg]
             deliver(2 * n + h, 2 * (yh * ZN + za) + core, h, chip)
 
+    def spread_out(n):
+        halves = differences(n)
+        za = (z + order[n]) % ZN
+        first = 2 * plan.paired + 4 * (n - plan.paired)
+        for h in range(YH):
+            m = first + 2 * h
+            for half in range(2):
+                msg[m + half] = halves[half][:, h * plan.msg:(h + 1) * plan.msg].astype(BF16)
+            if plan.direct and n == 7:
+                for half in range(2):
+                    pltpu.make_async_remote_copy(
+                        src_ref=msg.at[pl.ds(m, 2)], dst_ref=mir.at[row], send_sem=m_s, recv_sem=m_rs,
+                        device_id=(2 * (h * ZN + z) + half, yh * ZN + za), device_id_type=MESH).start()
+            for half in range(2):
+                deliver(m + half, 2 * (yh * ZN + za) + half, h, row)
+
+    def work(n):
+        if n < plan.paired:
+            compute(n)
+        else:
+            spread_out(n)
+
     def forward(step):
-        for part in range(2):
+        for part in range(plan.parts):
             for d in range(2):
                 arrival(d, step - 1, part).wait_recv()
-                if step < 3 or part == d:
+                if goes(d, step, part):
                     hop(d, step, part).start()
 
     hear(1)
@@ -332,31 +359,29 @@
     unpack(4)
     swap(1 - yh).wait_recv()
     expand(wblk.at[1 - yh], ex.at[4], wall.at[1 - yh])
-    compute(0)
-    compute(1)
+    for n in range(2):
+        work(n)
     forward(3)
     hear(4)
     tell(5)
+    waiting = list(range(plan.paired))
     for n in range(2, 7):
         if n > 4:
             unpack(n)
-        compute(n)
-        finish(n - 2)
+        work(n)
+        if waiting:
+            finish(waiting.pop(0))
+    for n in waiting:
+        finish(n)
     hear(5)
     tell(6)
-    finish(5)
-    finish(6)
-    for d in range(2):
-        arrival(d, 3, d).wait_recv()
+    hear(6)
+    for part in range(plan.parts):
+        for d in range(2):
+            if goes(d, 3, part):
+                arrival(d, 3, part).wait_recv()
     unpack(7)
-    halves = differences(7)
-    za = (z + order[7]) % ZN
-    for half in range(2):
-        total = halves[half].astype(BF16)
-        for h in range(YH):
-            m = 14 + 2 * half + h
-            msg[m] = total[:, h * plan.msg:(h + 1) * plan.msg]
-            deliver(m, 2 * (yh * ZN + za) + half, h, row)
+    work(7)
 
     def add_up(many):
         pltpu.make_async_copy(p2r.at[pl.ds(0, many)], p2r.at[pl.ds(0, many)], p2_rs).wait()
@@ -373,28 +398,46 @@
     def _():
         add_up(16)
 
-    hear(6)
     def mirror_copy(s):
         return pltpu.make_async_remote_copy(
             src_ref=tile, dst_ref=p3r.at[row % 2], send_sem=p3_s.at[s], recv_sem=p3_rs.at[row % 2],
             device_id=(2 * col + s, mirror_col), device_id_type=MESH)
 
-    for s in range(2):
-        self_mirror = (2 * col + s == row) & (mirror_col == col)
-
-        @pl.when(jnp.logical_not(self_mirror))
+    late_mirror = (gap == 4) if plan.direct else (gap < 0)
+
+    @pl.when(jnp.logical_not(late_mirror))
+    def _():
+        for s in range(2):
+            self_mirror = (2 * col + s == row) & (mirror_col == col)
+
+            @pl.when(jnp.logical_not(self_mirror))
+            def _():
+                mirror_copy(s).start()
+
+            @pl.when(self_mirror)
+            def _():
+                pltpu.make_async_copy(tile, p3r.at[s], p3_rs.at[s]).start()
+
+    base = dot(tile[...], zmat[...], NN)
+
+    if plan.direct:
+        @pl.when(late_mirror)
         def _():
-            mirror_copy(s).start()
-
-        @pl.when(self_mirror)
-        def _():
-            pltpu.make_async_copy(tile, p3r.at[s], p3_rs.at[s]).start()
-
-    base = dot(tile[...], zmat[...], NN)
+            pltpu.make_async_copy(mir, mir, m_rs).wait()
+            for s in range(2):
+                total = mir[0, s].astype(F32)
+                for n in range(1, 32):
+                    total = total + mir[n, s].astype(F32)
+                p3r[s] = total.astype(BF16)
+
+    @pl.when(jnp.logical_not(late_mirror))
+    def _():
+        for s in range(2):
+            pltpu.make_async_copy(p3r.at[s], p3r.at[s], p3_rs.at[s]).wait()
+
     br, bl = iota((32, 256), 0), iota((32, 256), 1)
     spread = None
     for s in range(2):
-        pltpu.make_async_copy(p3r.at[s], p3r.at[s], p3_rs.at[s]).wait()
         put = ((bl % 128) == br + NQ * s + SLOT * (bl // 128)) & (br < NQ)
         part = dot(p3r[s], jnp.where(put, 1.0, 0.0).astype(BF16), TN)
         spread = part if spread is None else spread + part
@@ -412,25 +455,28 @@
     for i in range(OW):
         out[i] = res[0:NQ, i * 256:i * 256 + NP * OW]
 
-    for part in range(2):
+    for part in range(plan.parts):
         for d in range(2):
             for step in range(4):
-                if step < 3 or part == d:
+                if goes(d, step, part):
                     hop(d, step, part).wait_send()
     swap(yh).wait_send()
-    for n in range(7):
+    for n in range(plan.paired):
         mate_copy(n).wait_send()
+
+    if plan.direct:
+        pltpu.make_async_copy(mir.at[pl.ds(0, 4)], mir.at[pl.ds(0, 4)], m_s).wait()
 
     @pl.when(home == yh)
     def _():
-        pltpu.make_async_copy(msg.at[pl.ds(0, 17)], msg.at[pl.ds(0, 17)], p2_s).wait()
+        pltpu.make_async_copy(msg.at[pl.ds(1, plan.messages - 1)], msg.at[pl.ds(1, plan.messages - 1)], p2_s).wait()
 
     @pl.when(home != yh)
     def _():
         pltpu.make_async_copy(msg, msg, p2_s).wait()
 
     for s in range(2):
-        @pl.when(jnp.logical_not((2 * col + s == row) & (mirror_col == col)))
+        @pl.when(jnp.logical_not(late_mirror | ((2 * col + s == row) & (mirror_col == col))))
         def _():
             mirror_copy(s).wait_send()
 
@@ -456,15 +502,16 @@
             pltpu.VMEM((ZN, OW * SLOT, plan.depth), BF16),
             pltpu.VMEM((YH, OW * SLOT, plan.depth), BF16),
             pltpu.VMEM((OW * SLOT, 512), F32),
-            pltpu.VMEM((ZN - 1, 32, YH * plan.msg), F32),
-            pltpu.VMEM((ZN - 1, 32, YH * plan.msg), BF16),
-            pltpu.VMEM((ZN - 1, 32, YH * plan.msg), BF16),
-            pltpu.VMEM((18, 32, plan.msg), BF16),
+            pltpu.VMEM((plan.paired, 32, YH * plan.msg), F32),
+            pltpu.VMEM((plan.paired, 32, YH * plan.msg), BF16),
+            pltpu.VMEM((plan.paired, 32, YH * plan.msg), BF16),
+            pltpu.VMEM((plan.messages, 32, plan.msg), BF16),
             pltpu.VMEM((32, 32, plan.msg), BF16),
             pltpu.VMEM((plan.msg, OW * 256), BF16),
             pltpu.VMEM((32, plan.msg), BF16),
             pltpu.VMEM((2, 32, plan.msg), BF16),
-            dma((16,)), dma((16,)), dma, dma, dma((ZN - 1,)), dma((ZN - 1,)), dma, dma, dma((2,)), dma((2,)),
+            dma((8 * plan.parts,)), dma((8 * plan.parts,)), dma, dma, dma((plan.paired,)), dma((plan.paired,)), dma, dma, dma((2,)), dma((2,)),
+            pltpu.VMEM((32 if plan.direct else 1, 2, 32, plan.msg), BF16), dma, dma,
             pltpu.SemaphoreType.REGULAR((28,)),
         ],
         name="cycle%d" % lanes,

time: 59.4 us -> 50.5 us (0.85)
  Pallas kernels: 55.6 us -> 47.1 us
    pallas_call x1, Pallas kernels: 55.6 us -> 47.1 us  [call(): pl.pallas_call(functools.partial(kernel, plan), out_shape=jax.ShapeDtypeS...]
where the time goes in v4:
time: 50.5 us; the launch traced here: 50.3 us
  Pallas kernels  47.1 us (93%)
  local copies, waits for them, and re-layouts  1.37 us (3%)
  other arithmetic  0.92 us (2%)
  between operations  0.67 us (1%)
    pallas_call x1, Pallas kernels, call(): pl.pallas_call(functools.partial(kernel, plan), out_shape=jax.ShapeDtypeS...  47.1 us

profile of v4, /device:TPU:7, one launch (start us, length us, event | category | flops | bytes accessed | tf_op | source)
XLA Modules:
  0.0 50.3 jit_solution(1858437031306506213)
XLA Ops:
  0.0 0.0 copy-start
  0.0 0.0 copy-start.2
  0.0 0.7 %copy-done = s32[64]{0:T(128)S(1)} copy-done((s32[64]{0:T(128)S(1)}, s32[64]{0:T(128)}, u32[]{:S(2)}) %copy-start) | copy-done | bytes 280
  0.7 0.1 pad_add_fusion
  0.7 0.1 broadcast_xor_fusion
  0.8 0.0 copy-done.2
  0.8 0.1 select_reduce_fusion
  0.9 0.0 copy-start.1
  0.9 0.7 %add_reduce_fusion = s32[]{:T(128)} fusion(s32[8]{0:T(128)S(1)} %select_reduce_fusion), kind=kLoop, calls=%fused_computation.24 | loop fusion | flops 583 | bytes 36 | tf_op jit(solution)/shard_map/reduce_max | solution.py:540
  1.6 0.0 copy-done.1
  2.2 47.4 %conditional.1 = (f32[4,25,200]{2,1,0:T(8,128)S(1)}) conditional(s32[]{:T(128)} %clamp.3, (s32[64]{0:T(128)S(1)}, bf16[25,50,256]{2,1,0:T(8,128)(2,1)}, bf16[25,50,256]{2,1,0:T(8,128)(2,1)}, s32[8]{0:T(128)S(1)}) %tuple.24, (s32[64]{0:T(128)S(1)}, bf16[25,50,256]{2,1,0:T(8,128)(2,1)}, bf16[25,50,256]{2,1,0:T(8,128)(2,1)}, ...), branch_computations={%region_2.3_spmd, %region_3.4_spmd, %region_4.5_spmd} | conditional | bytes 8 | solution.py:542
  2.3 47.1 %cycle64.1 = f32[4,25,200]{2,1,0:T(8,128)S(1)} custom-call(bf16[25,50,256]{2,1,0:T(8,128)(2,1)} %get-tuple-element.32.amps, bf16[25,50,256]{2,1,0:T(8,128)(2,1)} %get-tuple-element.34.integral, s32[1,64]{1,0:T(1,128)S(1)} %bitcast.12, s32[64]{0:T(128)S(1)} %get-tuple-element.35.occ, s32[8]{0:T(128)S(1)} %get-tuple-element.36.virt), custom_call_target="tpu_custom_call" | custom-call | tf_op jit(solution)/shard_map/cond/branch_0_fun/cycle64/pallas_call | solution.py:489
  49.6 0.7 %copy.9 = f32[4,25,200]{2,0,1:T(4,128)} copy(f32[4,25,200]{2,1,0:T(8,128)S(1)} %get-tuple-element.45) | data formatting | bytes 160000 | tf_op jit(solution)/shard_map/cond | solution.py:542
Async XLA Ops:
  0.0 0.7 %copy-start = (s32[64]{0:T(128)S(1)}, s32[64]{0:T(128)}, u32[]{:S(2)}) copy-start(s32[64]{0:T(128)} %param.11) | copy-start | bytes 772
  0.0 0.8 %copy-start.2 = (s32[64,5]{0,1:T(8,128)S(1)}, s32[64,5]{0,1:T(8,128)}, u32[]{:S(2)}) copy-start(s32[64,5]{0,1:T(8,128)} %constant.80) | copy-start | bytes 3844
  0.9 0.7 %copy-start.1 = (s32[8]{0:T(128)S(1)}, s32[8]{0:T(128)}, u32[]{:S(2)}) copy-start(s32[8]{0:T(128)} %param.10) | copy-start | bytes 100

commit v5 on v4

--- a/solution.py
+++ b/solution.py
@@ -244,10 +244,20 @@
         zmat[...] = (jnp.where(plus, 1.0, 0.0) - jnp.where(minus, 1.0, 0.0)).astype(BF16)
 
     low = iota((32, 128), 1) < SLOT
-    order = (0, ZN - 1, 1, ZN - 2, 2, ZN - 3, 3, 4)
-
-    def unpack(n):
-        za = (z + order[n]) % ZN
+
+    def source(n):
+        return (z + ZN + n // 2 - n % 2 * (2 * (n // 2) + 1)) % ZN
+
+    def each(first, many, *steps):
+        def body(k, carry):
+            for step in steps:
+                step(first + k, first)
+            return carry
+
+        lax.fori_loop(0, many, body, 0)
+
+    def unpack(n, first=0):
+        za = source(n)
         expand(blk.at[za], ex.at[za // 2], texp.at[n])
 
     def mate_copy(n):
@@ -256,7 +266,7 @@
             device_id_type=MESH)
 
     def differences(n):
-        za = (z + order[n]) % ZN
+        za = source(n)
         for h in range(YH):
             c32[:, h * 256:(h + 1) * 256] = dot(texp[n], wall[h], NT)
         la = virt[(yh * ZN + za) // 2]
@@ -303,22 +313,22 @@
             pltpu.make_async_copy(msg.at[m], p2r.at[place], p2_rs).start()
 
     def finish(n):
-        za = (z + order[n]) % ZN
+        za = source(n)
         mate_copy(n).wait_recv()
         total = (keep[n] + precv[n].astype(F32)).astype(BF16)
         for h in range(YH):
             msg[2 * n + h] = total[:, h * plan.msg:(h + 1) * plan.msg]
             deliver(2 * n + h, 2 * (yh * ZN + za) + core, h, chip)
 
-    def spread_out(n):
+    def spread_out(n, last):
         halves = differences(n)
-        za = (z + order[n]) % ZN
+        za = source(n)
         first = 2 * plan.paired + 4 * (n - plan.paired)
         for h in range(YH):
             m = first + 2 * h
             for half in range(2):
                 msg[m + half] = halves[half][:, h * plan.msg:(h + 1) * plan.msg].astype(BF16)
-            if plan.direct and n == 7:
+            if plan.direct and last:
                 for half in range(2):
                     pltpu.make_async_remote_copy(
                         src_ref=msg.at[pl.ds(m, 2)], dst_ref=mir.at[row], send_sem=m_s, recv_sem=m_rs,
@@ -326,11 +336,11 @@
             for half in range(2):
                 deliver(m + half, 2 * (yh * ZN + za) + half, h, row)
 
-    def work(n):
-        if n < plan.paired:
+    def work(n, first=0):
+        if first < plan.paired:
             compute(n)
         else:
-            spread_out(n)
+            spread_out(n, first == 7)
 
     def forward(step):
         for part in range(plan.parts):
@@ -346,32 +356,25 @@
     texp[...] = jnp.zeros(texp.shape, BF16)
     wall[...] = jnp.zeros(wall.shape, BF16)
     expand(wblk.at[yh], ex.at[z // 2], wall.at[yh])
-    unpack(0)
     hear(2)
     tell(3)
-    unpack(1)
-    unpack(2)
+    each(0, 3, unpack)
     forward(2)
     hear(3)
     tell(4)
     spread_matrix()
-    unpack(3)
-    unpack(4)
+    each(3, 2, unpack)
     swap(1 - yh).wait_recv()
     expand(wblk.at[1 - yh], ex.at[4], wall.at[1 - yh])
-    for n in range(2):
-        work(n)
+    each(0, 3, work)
     forward(3)
     hear(4)
     tell(5)
-    waiting = list(range(plan.paired))
-    for n in range(2, 7):
-        if n > 4:
-            unpack(n)
-        work(n)
-        if waiting:
-            finish(waiting.pop(0))
-    for n in waiting:
+    each(3, 2, work)
+    for n in range(min(3, plan.paired)):
+        finish(n)
+    each(5, 2, unpack, work)
+    for n in range(3, plan.paired):
         finish(n)
     hear(5)
     tell(6)
@@ -381,7 +384,7 @@
             if goes(d, 3, part):
                 arrival(d, 3, part).wait_recv()
     unpack(7)
-    work(7)
+    work(7, 7)
 
     def add_up(many):
         pltpu.make_async_copy(p2r.at[pl.ds(0, many)], p2r.at[pl.ds(0, many)], p2_rs).wait()
@@ -520,7 +523,7 @@
     )(amps, integral, occ_irrep.reshape(1, NO), occ_irrep, virt_irrep)
 
 
-TIERS = ((64, 32, 2), (96, 32, 4), (OW * NO, NO, 6))
+TIERS = ((64, 32, 2), (96, 32, 4), (128, 32, 6), (OW * NO, NO, 6))
 
 
 def shards(amps, integral, virt_irrep, occ_irrep):

time: 50.5 us -> 50 us (0.990)
  Pallas kernels: 47.1 us -> 46.4 us
    pallas_call x1, Pallas kernels: 47.1 us -> 46.4 us  [call(): pl.pallas_call(functools.partial(kernel, plan), out_shape=jax.ShapeDtypeS...]
where the time goes in v5:
time: 50 us; the launch traced here: 49.9 us
  Pallas kernels  46.4 us (93%)
  local copies, waits for them, and re-layouts  1.37 us (3%)
  other arithmetic  0.92 us (2%)
  between operations  0.67 us (1%)
    pallas_call x1, Pallas kernels, call(): pl.pallas_call(functools.partial(kernel, plan), out_shape=jax.ShapeDtypeS...  46.4 us

profile of v5, /device:TPU:7, one launch (start us, length us, event | category | flops | bytes accessed | tf_op | source)
XLA Modules:
  0.0 49.9 jit_solution(5232298833698885363)
XLA Ops:
  0.0 0.0 copy-start
  0.0 0.0 copy-start.2
  0.0 0.7 %copy-done = s32[64]{0:T(128)S(1)} copy-done((s32[64]{0:T(128)S(1)}, s32[64]{0:T(128)}, u32[]{:S(2)}) %copy-start) | copy-done | bytes 280
  0.7 0.1 pad_add_fusion
  0.7 0.1 broadcast_xor_fusion
  0.8 0.0 copy-done.2
  0.8 0.1 select_reduce_fusion
  0.9 0.0 copy-start.1
  0.9 0.7 %add_reduce_fusion = s32[]{:T(128)} fusion(s32[8]{0:T(128)S(1)} %select_reduce_fusion), kind=kLoop, calls=%fused_computation.25 | loop fusion | flops 631 | bytes 36 | tf_op jit(solution)/shard_map/reduce_max | solution.py:543
  1.6 0.0 copy-done.1
  2.2 46.9 %conditional.1 = (f32[4,25,200]{2,1,0:T(8,128)S(1)}) conditional(s32[]{:T(128)} %clamp.3, (s32[64]{0:T(128)S(1)}, bf16[25,50,256]{2,1,0:T(8,128)(2,1)}, bf16[25,50,256]{2,1,0:T(8,128)(2,1)}, s32[8]{0:T(128)S(1)}) %tuple.30, (s32[64]{0:T(128)S(1)}, bf16[25,50,256]{2,1,0:T(8,128)(2,1)}, bf16[25,50,256]{2,1,0:T(8,128)(2,1)}, ...), branch_computations={%region_2.3_spmd, %region_3.4_spmd, %region_4.5_spmd, %region_5.6_... | conditional | bytes 8 | solution.py:545
  2.3 46.4 %cycle64.1 = f32[4,25,200]{2,1,0:T(8,128)S(1)} custom-call(bf16[25,50,256]{2,1,0:T(8,128)(2,1)} %get-tuple-element.40.amps, bf16[25,50,256]{2,1,0:T(8,128)(2,1)} %get-tuple-element.42.integral, s32[1,64]{1,0:T(1,128)S(1)} %bitcast.14, s32[64]{0:T(128)S(1)} %get-tuple-element.44.occ, s32[8]{0:T(128)S(1)} %get-tuple-element.45.virt), custom_call_target="tpu_custom_call" | custom-call | tf_op jit(solution)/shard_map/cond/branch_0_fun/cycle64/pallas_call | solution.py:492
  49.1 0.7 %copy.9 = f32[4,25,200]{2,0,1:T(4,128)} copy(f32[4,25,200]{2,1,0:T(8,128)S(1)} %get-tuple-element.58) | data formatting | bytes 160000 | tf_op jit(solution)/shard_map/cond | solution.py:545
Async XLA Ops:
  0.0 0.7 %copy-start = (s32[64]{0:T(128)S(1)}, s32[64]{0:T(128)}, u32[]{:S(2)}) copy-start(s32[64]{0:T(128)} %param.12) | copy-start | bytes 772
  0.0 0.8 %copy-start.2 = (s32[64,5]{0,1:T(8,128)S(1)}, s32[64,5]{0,1:T(8,128)}, u32[]{:S(2)}) copy-start(s32[64,5]{0,1:T(8,128)} %constant.86) | copy-start | bytes 3844
  0.9 0.7 %copy-start.1 = (s32[8]{0:T(128)S(1)}, s32[8]{0:T(128)}, u32[]{:S(2)}) copy-start(s32[8]{0:T(128)} %param.11) | copy-start | bytes 100
